TPU v7x, 32 devices: a whole 2x2x4 slice. The times are simulated.
32 devices in a mesh: rows: 8 (over z, core), mem: 4 (over y, x).
Axes of the slice: x: 2, y: 2, z: 4, core: 2. Of those that a mesh axis runs over, the one named last changes fastest.
Arguments:
- ensemble_state: float32 [4096, 4096], P('rows', 'mem'), may hold values from -6 to 6
- predicted: float32 [3072, 4096], P('rows', 'mem'), may hold values from -6 to 6
- perturbed: float32 [3072, 4096], P('rows', 'mem'), may hold values from -9 to 9
- obs_variance: float32 [3, 256], replicated, may hold values from 0.25 to 4
- owners: int32 [3], replicated, may hold values from 0 to 7, as said below
- positions: int32 [3, 256], replicated, may hold values from 0 to 383, as said below
Outputs:
- analysis_state: float32 [4096, 4096], P('rows', 'mem')
- analysis_obs: float32 [3072, 4096], P('rows', 'mem')
Inputs may be any that keep to these rules, and one draw needn't show every extreme that they name: The 3 owners are distinct; the first and the last index of rows are always among them. Each batch's 256 positions are distinct; every batch holds position 0 and position 383.
All inputs are finite; a program needn't handle non-finite values.
Results may differ from a plain program's by a relative error of at most 0.0003.
Values sent between devices are 32-bit elements; how exact they have to be, the bound alone decides.
A program may use at most 64 MiB of HBM per device.

v0:
```python
import jax
import jax.numpy as jnp
from jax import lax
from jax.sharding import PartitionSpec as P

MEMBERS = 4096
BATCHES = 3


exact = lax.Precision.HIGHEST


def broadcast(array, axis, root):
    mine = lax.axis_index(axis) == root
    return lax.psum(jnp.where(mine, array, jnp.zeros_like(array)), axis)


def on_device(ensemble_state, predicted, perturbed, obs_variance, owners, positions):
    shard_rows = ensemble_state.shape[0]
    state_now = ensemble_state
    obs_now = predicted
    for number in range(BATCHES):
        root_index = owners[number]
        picked = positions[number]
        observed_local = jnp.take(obs_now, picked, axis=0)
        joined = jnp.concatenate([state_now, obs_now], axis=0)
        innovation_local = jnp.take(perturbed, picked, axis=0) - observed_local
        observed, innovation = (
            broadcast(observed_local, "rows", root_index),
            broadcast(innovation_local, "rows", root_index),
        )
        raw_cross = jnp.einsum("rm,pm->rp", joined, observed, precision=exact)
        joined_part = jnp.sum(joined, axis=1)
        obs_part = jnp.sum(observed, axis=1)
        raw_inner = jnp.einsum("qm,pm->qp", observed, observed, precision=exact)
        cross_total, inner_total, joined_sums, obs_sums = lax.psum(
            (raw_cross, raw_inner, joined_part, obs_part), "mem"
        )
        inner_cov = inner_total - obs_sums[:, None] * obs_sums[None, :] / MEMBERS
        cross_cov = cross_total - joined_sums[:, None] * obs_sums[None, :] / MEMBERS
        cross_cov = cross_cov / (MEMBERS - 1)
        inner_full = inner_cov / (MEMBERS - 1) + jnp.diag(obs_variance[number])
        factor = jnp.linalg.cholesky(inner_full)
        weights = jax.scipy.linalg.cho_solve((factor, True), innovation)
        updated = joined + jnp.dot(cross_cov, weights, precision=exact)
        state_now = updated[:shard_rows]
        obs_now = updated[shard_rows:]
    return (state_now, obs_now)


def solution(mesh):
    in_specs = (P("rows", "mem"), P("rows", "mem"), P("rows", "mem"), P(), P(), P())
    out_specs = (P("rows", "mem"), P("rows", "mem"))
    return jax.shard_map(
        on_device, mesh=mesh, in_specs=in_specs, out_specs=out_specs, check_vma=False
    )
```

profile of v0, /device:TPU:0, one launch (start us, length us, event | category | flops | bytes accessed | tf_op | source)
XLA Modules:
  0.0 643.8 jit_solution(16935366349603278020)
XLA Ops:
  22.6 63.0 %all-reduce.21.cloned.1.call-done = (f32[256,1024]{1,0:T(8,128)}, f32[256,1024]{1,0:T(8,128)}) async-done(((f32[256,1024]{1,0:T(8,128)}, f32[256,1024]{1,0:T(8,128)}), (f32[256,1024]{1,0:T(8,128)}, f32[256,1024]{1,0:T(8,128)})) %all-reduce.21.cloned.1.call-update) | async-done | bytes 2097168 | tf_op jit(solution)/shard_map/psum | solution.py:15
  89.0 6.3 fusion.86
  100.5 10.7 %all-reduce.6 = (f32[256]{0:T(256)S(1)}, f32[896]{0:T(1024)S(1)}) all-reduce(f32[256]{0:T(256)S(1)} %reduce_sum.55, f32[896]{0:T(1024)S(1)} %reduce_sum.54), channel_id=1, replica_groups=mesh['rows'=8,'mem'=4] {'mem'}, use_global_device_ids=true, to_apply=%region_5.7 | all-reduce | flops 1152 | bytes 9216 | tf_op jit(solution)/shard_map/psum | solution.py:36
  111.2 38.9 %all-reduce.27.cloned.1.call-done = (f32[256,256]{0,1:T(8,128)}, f32[896,256]{1,0:T(8,128)}) async-done(((f32[256,256]{0,1:T(8,128)}, f32[896,256]{1,0:T(8,128)}), (f32[256,256]{0,1:T(8,128)}, f32[896,256]{1,0:T(8,128)})) %all-reduce.27.cloned.1.call-update) | async-done | bytes 1179664 | tf_op jit(solution)/shard_map/psum | solution.py:36
  152.4 11.7 %cholesky.172 = f32[128,128]{1,0:T(8,128)S(1)} custom-call(f32[128,128]{1,0:T(8,128)S(1)} %cholesky.270), custom_call_target="Cholesky" | custom-call | tf_op jit(solution)/shard_map/jit(cholesky)/cholesky | solution.py:43
  164.2 9.8 %custom-call.17 = f32[1,128,128]{1,2,0:T(8,128)S(1)} custom-call(f32[1,128,128]{2,1,0:T(8,128)S(1)} %get-tuple-element.93), custom_call_target="InvertDiagBlocksLowerTriangular" | custom-call | tf_op jit(solution)/shard_map/jit(cholesky)/cholesky | solution.py:43
  174.5 11.7 %cholesky.189 = f32[128,128]{1,0:T(8,128)S(1)} custom-call(f32[128,128]{1,0:T(8,128)S(1)} %convolution_subtract_fusion.8), custom_call_target="Cholesky" | custom-call | tf_op jit(solution)/shard_map/jit(cholesky)/cholesky | solution.py:43
  192.6 19.7 %custom-call.18 = f32[2,128,128]{1,2,0:T(8,128)S(1)} custom-call(f32[2,128,128]{2,1,0:T(8,128)S(1)} %get-tuple-element.25), custom_call_target="InvertDiagBlocksLowerTriangular" | custom-call | tf_op jit(solution)/shard_map/jit(_cho_solve)/triangular_solve | solution.py:44
  228.9 64.9 %all-reduce.19.cloned.1.call-done = (f32[256,1024]{1,0:T(8,128)}, f32[256,1024]{1,0:T(8,128)}) async-done(((f32[256,1024]{1,0:T(8,128)}, f32[256,1024]{1,0:T(8,128)}), (f32[256,1024]{1,0:T(8,128)}, f32[256,1024]{1,0:T(8,128)})) %all-reduce.19.cloned.1.call-update) | async-done | bytes 2097168 | tf_op jit(solution)/shard_map/psum | solution.py:15
  297.1 6.3 fusion.88
  306.3 10.8 %all-reduce.5 = (f32[256]{0:T(256)S(1)}, f32[896]{0:T(1024)S(1)}) all-reduce(f32[256]{0:T(256)S(1)} %reduce_sum.57, f32[896]{0:T(1024)S(1)} %get-tuple-element.105), channel_id=1, replica_groups=mesh['rows'=8,'mem'=4] {'mem'}, use_global_device_ids=true, to_apply=%region_17.21 | all-reduce | flops 1152 | bytes 9216 | tf_op jit(solution)/shard_map/psum | solution.py:36
  317.1 41.0 %all-reduce.25.cloned.1.call-done = (f32[256,256]{0,1:T(8,128)}, f32[896,256]{1,0:T(8,128)}) async-done(((f32[256,256]{0,1:T(8,128)}, f32[896,256]{1,0:T(8,128)}), (f32[256,256]{0,1:T(8,128)}, f32[896,256]{1,0:T(8,128)})) %all-reduce.25.cloned.1.call-update) | async-done | bytes 1179664 | tf_op jit(solution)/shard_map/psum | solution.py:36
  360.4 11.7 %cholesky.206 = f32[128,128]{1,0:T(8,128)S(1)} custom-call(f32[128,128]{1,0:T(8,128)S(1)} %cholesky.273), custom_call_target="Cholesky" | custom-call | tf_op jit(solution)/shard_map/jit(cholesky)/cholesky | solution.py:43
  372.2 9.8 %custom-call.19 = f32[1,128,128]{1,2,0:T(8,128)S(1)} custom-call(f32[1,128,128]{2,1,0:T(8,128)S(1)} %get-tuple-element.89), custom_call_target="InvertDiagBlocksLowerTriangular" | custom-call | tf_op jit(solution)/shard_map/jit(cholesky)/cholesky | solution.py:43
  382.5 11.7 %cholesky.223 = f32[128,128]{1,0:T(8,128)S(1)} custom-call(f32[128,128]{1,0:T(8,128)S(1)} %convolution_subtract_fusion.7), custom_call_target="Cholesky" | custom-call | tf_op jit(solution)/shard_map/jit(cholesky)/cholesky | solution.py:43
  401.2 19.7 %custom-call.20 = f32[2,128,128]{1,2,0:T(8,128)S(1)} custom-call(f32[2,128,128]{2,1,0:T(8,128)S(1)} %get-tuple-element.26), custom_call_target="InvertDiagBlocksLowerTriangular" | custom-call | tf_op jit(solution)/shard_map/jit(_cho_solve)/triangular_solve | solution.py:44
  435.2 64.9 %all-reduce.17.cloned.1.call-done = (f32[256,1024]{1,0:T(8,128)}, f32[256,1024]{1,0:T(8,128)}) async-done(((f32[256,1024]{1,0:T(8,128)}, f32[256,1024]{1,0:T(8,128)}), (f32[256,1024]{1,0:T(8,128)}, f32[256,1024]{1,0:T(8,128)})) %all-reduce.17.cloned.1.call-update) | async-done | bytes 2097168 | tf_op jit(solution)/shard_map/psum | solution.py:15
  503.5 6.4 fusion.90
  510.1 11.0 %all-reduce.4 = (f32[256]{0:T(256)S(1)}, f32[896]{0:T(1024)S(1)}) all-reduce(f32[256]{0:T(256)S(1)} %reduce_sum.59, f32[896]{0:T(1024)S(1)} %get-tuple-element.109), channel_id=1, replica_groups=mesh['rows'=8,'mem'=4] {'mem'}, use_global_device_ids=true, to_apply=%region_25.29 | all-reduce | flops 1152 | bytes 9216 | tf_op jit(solution)/shard_map/psum | solution.py:36
  521.1 43.3 %all-reduce.23.cloned.1.call-done = (f32[256,256]{0,1:T(8,128)}, f32[896,256]{1,0:T(8,128)}) async-done(((f32[256,256]{0,1:T(8,128)}, f32[896,256]{1,0:T(8,128)}), (f32[256,256]{0,1:T(8,128)}, f32[896,256]{1,0:T(8,128)})) %all-reduce.23.cloned.1.call-update) | async-done | bytes 1179664 | tf_op jit(solution)/shard_map/psum | solution.py:36
  566.7 11.7 %cholesky.240 = f32[128,128]{1,0:T(8,128)S(1)} custom-call(f32[128,128]{1,0:T(8,128)S(1)} %cholesky.276), custom_call_target="Cholesky" | custom-call | tf_op jit(solution)/shard_map/jit(cholesky)/cholesky | solution.py:43
  578.5 9.8 %custom-call.21 = f32[1,128,128]{1,2,0:T(8,128)S(1)} custom-call(f32[1,128,128]{2,1,0:T(8,128)S(1)} %get-tuple-element.85), custom_call_target="InvertDiagBlocksLowerTriangular" | custom-call | tf_op jit(solution)/shard_map/jit(cholesky)/cholesky | solution.py:43
  588.8 11.7 %cholesky.257 = f32[128,128]{1,0:T(8,128)S(1)} custom-call(f32[128,128]{1,0:T(8,128)S(1)} %convolution_subtract_fusion.6), custom_call_target="Cholesky" | custom-call | tf_op jit(solution)/shard_map/jit(cholesky)/cholesky | solution.py:43
  607.3 19.7 %custom-call.22 = f32[2,128,128]{1,2,0:T(8,128)S(1)} custom-call(f32[2,128,128]{2,1,0:T(8,128)S(1)} %get-tuple-element.27), custom_call_target="InvertDiagBlocksLowerTriangular" | custom-call | tf_op jit(solution)/shard_map/jit(_cho_solve)/triangular_solve | solution.py:44
  (162 shorter events, 108.6 us)
Async XLA Ops:
  7.2 5.3 copy-start
  7.2 78.5 %all-reduce.21.cloned.1.call-start = ((), (), s32[]{:S(2)}) async-start(), calls=%async_computation.2 | async-start | bytes 4194304 | tf_op jit(solution)/shard_map/psum | solution.py:15
  18.0 3.4 copy-start.2
  18.0 132.1 %all-reduce.27.cloned.1.call-start = ((), (), s32[]{:S(2)}) async-start(), calls=%async_computation.5 | async-start | bytes 2359296 | tf_op jit(solution)/shard_map/psum | solution.py:36
  95.3 198.4 %all-reduce.19.cloned.1.call-start = ((), (), s32[]{:S(2)}) async-start(), calls=%async_computation.1 | async-start | bytes 4194304 | tf_op jit(solution)/shard_map/psum | solution.py:15
  98.3 2.1 copy-start.17
  98.3 2.1 copy-start.7
  100.5 111.8 %copy-start.11 = (f32[256,1024]{1,0:T(8,128)S(1)}, f32[256,1024]{1,0:T(8,128)}, u32[]{:S(2)}) copy-start(f32[256,1024]{1,0:T(8,128)} %get-tuple-element.56) | copy-start | bytes 3145732
  212.3 3.7 copy-start.15
  221.7 1.8 copy-start.5
  228.8 129.3 %all-reduce.25.cloned.1.call-start = ((), (), s32[]{:S(2)}) async-start(), calls=%async_computation.4 | async-start | bytes 2359296 | tf_op jit(solution)/shard_map/psum | solution.py:36
  303.4 196.7 %all-reduce.17.cloned.1.call-start = ((), (), s32[]{:S(2)}) async-start(), calls=%async_computation | async-start | bytes 4194304 | tf_op jit(solution)/shard_map/psum | solution.py:15
  304.2 2.0 copy-start.8
  306.3 114.6 %copy-start.12 = (f32[256,1024]{1,0:T(8,128)S(1)}, f32[256,1024]{1,0:T(8,128)}, u32[]{:S(2)}) copy-start(f32[256,1024]{1,0:T(8,128)} %get-tuple-element.54) | copy-start | bytes 3145732
  420.9 3.7 copy-start.6
  420.9 3.7 copy-start.16
  428.4 1.8 copy-start.3
  430.3 2.0 copy-start.10
  435.2 129.2 %all-reduce.23.cloned.1.call-start = ((), (), s32[]{:S(2)}) async-start(), calls=%async_computation.3 | async-start | bytes 2359296 | tf_op jit(solution)/shard_map/psum | solution.py:36
  503.5 6.4 copy-start.9
  509.9 117.1 %copy-start.13 = (f32[256,1024]{1,0:T(8,128)S(1)}, f32[256,1024]{1,0:T(8,128)}, u32[]{:S(2)}) copy-start(f32[256,1024]{1,0:T(8,128)} %get-tuple-element.52) | copy-start | bytes 3145732
  627.0 3.7 copy-start.4
  627.0 3.7 copy-start.14
  630.8 6.0 copy-start.1
Sparse Core Ops, SparseCore 0:
  18.1 67.4 all-reduce.20
  95.4 54.6 all-reduce.26
  228.9 64.7 all-reduce.18
  303.5 54.5 all-reduce.24
  435.3 64.7 all-reduce.16
  510.0 54.3 all-reduce.22
where the time goes:
time: 651 us; the launch traced here: 644 us
  waiting for transfers between devices  316 us (49%)
  other arithmetic  180 us (28%)
  matrix products  54.1 us (8%)
  local copies, waits for them, and re-layouts  39 us (6%)
  blocking collectives  32.5 us (5%)
  between operations  20.9 us (3%)
    psum x3, waiting for transfers between devices, broadcast(): return lax.psum(jnp.where(mine, array, jnp.zeros_like(array)), axis)  193 us
    psum x3, waiting for transfers between devices, on_device(): lax.psum((raw_cross, raw_inner, joined_part, obs_part), 'mem')  123 us
    another operation x20, other arithmetic, on_device(): factor = jnp.linalg.cholesky(inner_full)  103 us
    another operation x7, other arithmetic, on_device(): weights = jax.scipy.linalg.cho_solve((factor, True), innovation)  59.1 us
    psum x3, blocking collectives, on_device(): lax.psum((raw_cross, raw_inner, joined_part, obs_part), 'mem')  32.5 us
    dot_general x3, matrix products, on_device(): raw_cross = jnp.einsum('rm,pm->rp', joined, observed, precision=exact)  19 us
  transfers between devices with their start and end apart: 6, of which 6 were waited for; matrix products, arithmetic and copies ran while one was open for 2% of the time, Pallas kernels for 0%

commit v1 on v0

v1 whole, which is shorter than its diff:
```python
import jax
import jax.numpy as jnp
from jax import lax
from jax.experimental import pallas as pl
from jax.experimental.pallas import tpu as pltpu
from jax.sharding import PartitionSpec as P

exact = lax.Precision.HIGHEST
good = lax.Precision.HIGH


def invert_kernel(a_ref, o_ref):
    size = a_ref.shape[0]
    width = 32
    o_ref[...] = a_ref[...]
    lane = lax.broadcasted_iota(jnp.int32, (width, size), 1)
    sub = lax.broadcasted_iota(jnp.int32, (width, size), 0)
    lanes = lax.broadcasted_iota(jnp.int32, (size, size), 1)
    for first in range(0, size, width):
        block = o_ref[first:first + width, :]
        side = o_ref[:, first:first + width]
        for i in range(width):
            k = first + i
            inv = 1.0 / block[i:i + 1, k:k + 1]
            row = jnp.where(lane[:1] == k, 1.0, block[i:i + 1, :]) * inv
            col = block[:, k:k + 1]
            rest = jnp.where(lane == k, 0.0, block) - col * row
            block = jnp.where(sub == i, row, rest)
        inside = (lanes >= first) & (lanes < first + width)
        o_ref[...] = jnp.where(inside, 0.0, o_ref[...]) - jnp.dot(
            side, block, precision=exact, preferred_element_type=jnp.float32
        )
        o_ref[first:first + width, :] = block


def invert(matrix):
    return pl.pallas_call(
        invert_kernel,
        out_shape=jax.ShapeDtypeStruct(matrix.shape, jnp.float32),
        in_specs=[pl.BlockSpec(memory_space=pltpu.VMEM)],
        out_specs=pl.BlockSpec(memory_space=pltpu.VMEM),
        cost_estimate=pl.CostEstimate(
            flops=30_000_000_000, bytes_accessed=2 * matrix.size * 4, transcendentals=0
        ),
    )(matrix)


def outer(a, b, precision=good):
    return lax.dot_general(
        a, b, (((1,), (1,)), ((), ())), precision=precision,
        preferred_element_type=jnp.float32,
    )


def times(a, b):
    return jnp.dot(a, b, precision=good, preferred_element_type=jnp.float32)


def spread(pairs, owners):
    me = lax.axis_index("rows")
    masked = [
        jnp.where(owners[number] == me, pair, 0.0) for number, pair in enumerate(pairs)
    ]
    return lax.psum(masked, "rows")


def on_device(members, state, obs, perturbed, obs_variance, owners, positions):
    batches, psize = positions.shape
    pairs = []
    for number in range(batches):
        picked = positions[number]
        seen = obs.at[picked].get(mode="promise_in_bounds")
        wanted = perturbed.at[picked].get(mode="promise_in_bounds")
        pairs.append(jnp.concatenate([seen, wanted - seen], axis=0))
    pairs = spread(pairs, owners)
    anomaly = jnp.concatenate([pair[:psize] for pair in pairs], axis=0)
    innovation = jnp.concatenate([pair[psize:] for pair in pairs], axis=0)
    obs_sum = jnp.sum(anomaly, axis=1).reshape(batches, psize)
    inn_sum = jnp.sum(innovation, axis=1).reshape(batches, psize)
    packed = jnp.concatenate(
        [outer(anomaly, anomaly[:psize], exact), obs_sum, inn_sum], axis=0
    )
    packed = lax.psum(packed, "mem")
    total = batches * psize
    obs_sum = packed[total:total + batches].reshape(total, 1)
    inn_mean = packed[total + batches:].reshape(total, 1) / members
    gram = packed[:total] - obs_sum * obs_sum[:psize].reshape(1, psize) / members
    anomaly = anomaly - obs_sum / members
    for number in range(batches):
        gram = gram / (members - 1)
        inner = gram[:psize] + jnp.diag(obs_variance[number])
        now = anomaly[:psize]
        raw = (outer(state, now), outer(obs, now))
        cross_state, cross_obs = lax.psum(raw, "mem")
        inverse = invert(inner)
        weights = times(inverse, innovation[:psize])
        cross_state, cross_obs, weights, inverse = lax.optimization_barrier(
            (cross_state, cross_obs, weights, inverse)
        )
        if number + 1 < batches:
            mean_weight = jnp.dot(inverse, inn_mean[:psize], precision=exact)
            ahead = gram[psize:]
            change = times(ahead, weights)
            shift = jnp.dot(ahead, mean_weight, precision=exact)
            anomaly = anomaly[psize:] + (change - shift)
            innovation = innovation[psize:] - change
            inn_mean = inn_mean[psize:] - shift
            gram = lax.psum(outer(anomaly, anomaly[:psize], exact), "mem")
        state = state + times(cross_state / (members - 1), weights)
        obs = obs + times(cross_obs / (members - 1), weights)
    return state, obs


def solution(mesh):
    in_specs = (P("rows", "mem"), P("rows", "mem"), P("rows", "mem"), P(), P(), P())
    out_specs = (P("rows", "mem"), P("rows", "mem"))

    def whole(*args):
        members = args[0].shape[1]

        def body(*local):
            return on_device(members, *local)

        return jax.shard_map(
            body, mesh=mesh, in_specs=in_specs, out_specs=out_specs, check_vma=False
        )(*args)

    return whole
```

time: 651 us -> 530 us (0.81)
  other arithmetic: 180 us -> 18.8 us
  Pallas kernels: 0 us -> 80.7 us
  blocking collectives: 32.5 us -> 0 us
  local copies, waits for them, and re-layouts: 39 us -> 23.7 us
  waiting for transfers between devices: 316 us -> 325 us
    another operation x27 -> x0, other arithmetic: 162 us -> none  [the longest x20 103 us: on_device(): factor = jnp.linalg.cholesky(inner_full)]
    pallas_call x0 -> x3, Pallas kernels: none -> 80.7 us  [invert(): pl.pallas_call(invert_kernel, out_shape=jax.ShapeDtypeStruct(matrix.shape...]
    psum x3 -> x0, blocking collectives: 32.5 us -> none  [on_device(): lax.psum((raw_cross, raw_inner, joined_part, obs_part), 'mem')]
    dot_general x9 -> x24, matrix products: 41.8 us -> 55.8 us  [the longest x11 31.6 us: times(): return jnp.dot(a, b, precision=good, preferred_element_type=jnp.float32)]
    another operation x24 -> x0, matrix products: 12.3 us -> none  [the longest x18 10.9 us: on_device(): weights = jax.scipy.linalg.cho_solve((factor, True), innovation)]
    another operation x28 -> x0, local copies, waits for them, and re-layouts: 12 us -> none  [the longest x22 11.9 us: on_device(): weights = jax.scipy.linalg.cho_solve((factor, True), innovation)]
    psum x6 -> x5, waiting for transfers between devices: 316 us -> 325 us  [the longest x1 140 us: spread(): return lax.psum(masked, 'rows')]
  transfers between devices with their start and end apart: 6 -> 5, of which waited for: 6 -> 5; matrix products, arithmetic and copies ran while one was open for 2% -> 0% of each run, Pallas kernels for 0% -> 5%
where the time goes in v1:
time: 530 us; the launch traced here: 521 us
  waiting for transfers between devices  325 us (61%)
  Pallas kernels  80.7 us (15%)
  matrix products  55.8 us (11%)
  local copies, waits for them, and re-layouts  23.7 us (4%)
  other arithmetic  18.8 us (4%)
  between operations  16.4 us (3%)
    psum x1, waiting for transfers between devices, spread(): return lax.psum(masked, 'rows')  140 us
    psum x3, waiting for transfers between devices, on_device(): cross_state, cross_obs = lax.psum(raw, 'mem')  137 us
    pallas_call x3, Pallas kernels, invert(): pl.pallas_call(invert_kernel, out_shape=jax.ShapeDtypeStruct(matrix.shape...  80.7 us
    psum x1, waiting for transfers between devices, on_device(): packed = lax.psum(packed, 'mem')  49.1 us
    dot_general x11, matrix products, times(): return jnp.dot(a, b, precision=good, preferred_element_type=jnp.float32)  31.6 us
    dot_general x9, matrix products, outer(): lax.dot_general(a, b, (((1,), (1,)), ((), ())), precision=precision, pref...  21.7 us
  transfers between devices with their start and end apart: 5, of which 5 were waited for; matrix products, arithmetic and copies ran while one was open for 0% of the time, Pallas kernels for 5%

profile of v1, /device:TPU:0, one launch (start us, length us, event | category | flops | bytes accessed | tf_op | source)
XLA Modules:
  0.0 521.2 jit_solution(11654089748987055146)
XLA Ops:
  8.1 3.9 gather_fusion.2
  12.0 2.0 gather_fusion.3
  14.1 2.0 gather_fusion
  16.1 2.0 gather_fusion.1
  18.1 2.0 gather_fusion.4
  32.8 139.6 %all-reduce.12.cloned.1.call-done = (f32[512,1024]{1,0:T(8,128)}, f32[512,1024]{1,0:T(8,128)}, f32[512,1024]{1,0:T(8,128)}) async-done(((f32[512,1024]{1,0:T(8,128)}, f32[512,1024]{1,0:T(8,128)}, f32[512,1024]{1,0:T(8,128)}), (f32[512,1024]{1,0:T(8,128)}, f32[512,1024]{1,0:T(8,128)}, f32[512,1024]{1,0:T(8,128)})) %all-reduce.12.cloned.1.call-update) | async-done | bytes 6291472 | tf_op jit(solution)/shard_map/psum | solution.py:64
  176.9 3.5 fusion.2
  180.7 2.1 pad_maximum_fusion.2
  182.9 49.1 %all-reduce.10.cloned.1.call-done = f32[774,256]{1,0:T(8,128)} async-done(((f32[774,256]{1,0:T(8,128)}), f32[774,256]{1,0:T(8,128)}) %all-reduce.10.cloned.1.call-update) | async-done | bytes 792592 | tf_op jit(solution)/shard_map/psum | solution.py:83
  232.8 3.4 fusion
  236.2 3.1 convolution_bitcast_fusion.1
  239.3 3.2 convolution_bitcast_fusion
  244.7 26.9 %shard_map.77 = f32[256,256]{1,0:T(8,128)} custom-call(f32[256,256]{1,0:T(8,128)} %slice_add_fusion.3.a_ref), custom_call_target="tpu_custom_call" | custom-call | flops 30000001024 | bytes 524288 | tf_op jit(solution)/shard_map/pallas_call | solution.py:37
  273.5 22.3 %all-reduce.18.cloned.1.call-done = (f32[512,256]{1,0:T(8,128)}, f32[384,256]{0,1:T(8,128)}) async-done(((f32[512,256]{1,0:T(8,128)}, f32[384,256]{0,1:T(8,128)}), (f32[512,256]{1,0:T(8,128)}, f32[384,256]{0,1:T(8,128)})) %all-reduce.18.cloned.1.call-update) | async-done | bytes 917520 | tf_op jit(solution)/shard_map/psum | solution.py:94
  297.7 4.9 maximum_subtract_fusion
  302.6 2.7 fusion.8
  305.3 11.7 %convolution_add_fusion.5 = f32[384,1024]{1,0:T(8,128)S(1)} fusion(f32[384,1024]{1,0:T(8,128)S(1)} %copy-done.2, f32[256,1024]{1,0:T(8,128)S(1)} %fusion.43, f32[384,256]{0,1:T(8,128)S(1)} %copy-done.35), kind=kOutput, calls=%fused_computation.21 | convolution fusion | flops 604471296 | bytes 4587520 | tf_op jit(solution)/shard_map/dot_general | solution.py:56
  323.0 59.2 %all-reduce.16.cloned.1.call-done = (f32[512,256]{1,0:T(8,128)}, f32[384,256]{0,1:T(8,128)}, f32[512,256]{1,0:T(8,128)}) async-done(((f32[512,256]{1,0:T(8,128)}, f32[384,256]{0,1:T(8,128)}, f32[512,256]{1,0:T(8,128)}), (f32[512,256]{1,0:T(8,128)}, f32[384,256]{0,1:T(8,128)}, f32[512,256]{1,0:T(8,128)})) %all-reduce.16.cloned.1.call-update) | async-done | bytes 1441808 | tf_op jit(solution)/shard_map/psum | solution.py:94
  384.2 26.9 %shard_map.78 = f32[256,256]{1,0:T(8,128)} custom-call(f32[256,256]{1,0:T(8,128)} %slice_add_fusion.2.a_ref), custom_call_target="tpu_custom_call" | custom-call | flops 30000001024 | bytes 524288 | tf_op jit(solution)/shard_map/pallas_call | solution.py:37
  411.1 2.0 fusion.4
  424.1 55.1 %all-reduce.14.cloned.1.call-done = (f32[512,256]{1,0:T(8,128)}, f32[384,256]{0,1:T(8,128)}, f32[256,256]{1,0:T(8,128)}) async-done(((f32[512,256]{1,0:T(8,128)}, f32[384,256]{0,1:T(8,128)}, f32[256,256]{1,0:T(8,128)}), (f32[512,256]{1,0:T(8,128)}, f32[384,256]{0,1:T(8,128)}, f32[256,256]{1,0:T(8,128)})) %all-reduce.14.cloned.1.call-update) | async-done | bytes 1179664 | tf_op jit(solution)/shard_map/psum | solution.py:94
  481.0 27.0 %shard_map.79 = f32[256,256]{1,0:T(8,128)} custom-call(f32[256,256]{1,0:T(8,128)} %select_add_fusion.a_ref), custom_call_target="tpu_custom_call" | custom-call | flops 30000001024 | bytes 524288 | tf_op jit(solution)/shard_map/pallas_call | solution.py:37
  509.7 2.4 convolution_add_fusion
  512.2 2.1 convolution_add_fusion.3
  (136 shorter events, 45.7 us)
Async XLA Ops:
  7.2 4.9 copy-start
  7.2 165.2 %all-reduce.12.cloned.1.call-start = ((), (), s32[]{:S(2)}) async-start(), calls=%async_computation.1 | async-start | bytes 12582912 | tf_op jit(solution)/shard_map/psum | solution.py:64
  22.1 4.1 copy-start.15
  32.8 199.2 %all-reduce.10.cloned.1.call-start = ((), (), s32[]{:S(2)}) async-start(), calls=%async_computation | async-start | bytes 1589248 | tf_op jit(solution)/shard_map/psum | solution.py:83
  172.4 2.9 copy-start.28
  174.2 6.2 %copy-start.16 = (f32[256,1024]{1,0:T(8,128)}, f32[256,1024]{1,0:T(8,128)S(1)}, u32[]{:S(2)}) copy-start(f32[256,1024]{1,0:T(8,128)S(1)} %get-tuple-element.41) | copy-start | bytes 3145732
  175.9 4.5 copy-start.18
  175.9 4.5 copy-start.19
  182.8 113.0 %all-reduce.18.cloned.1.call-start = ((), (), s32[]{:S(2)}) async-start(), calls=%async_computation.4 | async-start | bytes 1835008 | tf_op jit(solution)/shard_map/psum | solution.py:94
  236.2 3.1 copy-start.20
  239.3 3.2 copy-start.31
  239.3 3.2 slice-start
  244.4 137.9 %all-reduce.16.cloned.1.call-start = ((), (), s32[]{:S(2)}) async-start(), calls=%async_computation.3 | async-start | bytes 2883584 | tf_op jit(solution)/shard_map/psum | solution.py:94
  271.5 24.3 %copy-start.29 = (f32[256,256]{1,0:T(8,128)S(1)}, f32[256,256]{1,0:T(8,128)}, u32[]{:S(2)}) copy-start(f32[256,256]{1,0:T(8,128)} %shard_map.77) | copy-start | bytes 786436
  273.5 31.8 %copy-start.7 = (f32[256,1024]{1,0:T(8,128)}, f32[256,1024]{1,0:T(8,128)S(1)}, u32[]{:S(2)}) copy-start(f32[256,1024]{1,0:T(8,128)S(1)} %fusion.43) | copy-start | bytes 3145732
  302.6 18.5 %copy-start.3 = (f32[512,1024]{1,0:T(8,128)}, f32[512,1024]{1,0:T(8,128)S(1)}, u32[]{:S(2)}) copy-start(f32[512,1024]{1,0:T(8,128)S(1)} %get-tuple-element.36) | copy-start | bytes 6291460
  302.6 2.7 copy-start.35
  305.3 14.7 %copy-start.21 = (f32[512,1024]{1,0:T(8,128)S(1)}, f32[512,1024]{1,0:T(8,128)}, u32[]{:S(2)}) copy-start(f32[512,1024]{1,0:T(8,128)} %param.6) | copy-start | bytes 6291460
  323.0 156.3 %all-reduce.14.cloned.1.call-start = ((), (), s32[]{:S(2)}) async-start(), calls=%async_computation.2 | async-start | bytes 2359296 | tf_op jit(solution)/shard_map/psum | solution.py:94
  383.3 32.3 %copy-start.27 = (f32[512,256]{1,0:T(8,128)}, f32[512,256]{1,0:T(8,128)S(1)}, u32[]{:S(2)}) copy-start(f32[512,256]{1,0:T(8,128)S(1)} %broadcast_multiply_fusion) | copy-start | bytes 1572868
  414.2 6.0 %copy-start.9 = (f32[384,1024]{1,0:T(8,128)}, f32[384,1024]{1,0:T(8,128)S(1)}, u32[]{:S(2)}) copy-start(f32[384,1024]{1,0:T(8,128)S(1)} %convolution_add_fusion.4) | copy-start | bytes 4718596
  415.3 6.9 %copy-start.5 = (f32[512,1024]{1,0:T(8,128)}, f32[512,1024]{1,0:T(8,128)S(1)}, u32[]{:S(2)}) copy-start(f32[512,1024]{1,0:T(8,128)S(1)} %convolution_add_fusion.1) | copy-start | bytes 6291460
  481.0 27.0 %copy-start.22 = (f32[512,1024]{1,0:T(8,128)S(1)}, f32[512,1024]{1,0:T(8,128)}, u32[]{:S(2)}) copy-start(f32[512,1024]{1,0:T(8,128)} %get-tuple-element.35) | copy-start | bytes 6291460
  509.7 4.5 copy-start.1
  (22 other events, 40.3 us)
Sparse Core Ops, SparseCore 0:
  32.9 139.4 all-reduce.11
  182.9 49.0 all-reduce.9
  244.5 51.2 all-reduce.17
  323.1 59.1 all-reduce.15
  424.2 54.9 all-reduce.13
